TPU v7x, 256 devices: a whole 4x4x8 slice. The times are simulated.
256 devices in a mesh: dp: 32 (over y, z), mp: 8 (over x, core).
Axes of the slice: x: 4, y: 4, z: 8, core: 2. Of those that a mesh axis runs over, the one named last changes fastest.
Arguments:
- tokens: bfloat16 [4096, 8192], P('dp'), may hold values from -6 to 6
- rotation: float32 [8192, 8192], P('dp', 'mp'), may hold values from -6 to 6
- key_weight: bfloat16 [8192, 1024], P('dp', 'mp'), may hold values from -0.125 to 0.125
- grad_out: bfloat16 [4096, 1024], P('dp', 'mp'), may hold values from -6 to 6
Outputs:
- projected: bfloat16 [4096, 1024], P('dp', 'mp')
- new_panel: float32 [8192, 128], P('dp', 'mp')
All inputs are finite; a program needn't handle non-finite values.
Results may differ from a plain program's by a relative error of at most 0.014.
Values may be sent and summed in bfloat16 or wider, within the bound.
No kernel may reach another device: no remote copies, remote signals or barrier semaphores. Data moves between devices by JAX's collectives and lax.ppermute only.
A program may use at most 128 MiB of HBM per device.

v0:
```python
import jax
import jax.numpy as jnp
from jax import lax
from jax.sharding import PartitionSpec as P

D = 8192
PANEL = 128
ITERS = 2


STEP_GAIN = 0.8
LEVELS = 7.0
HIGHEST_PRECISION = lax.Precision.HIGHEST
CONTRACT_ROWS = (((0,), (0,)), ((), ()))
CONTRACT_COLUMNS = (((1,), (1,)), ((), ()))


def soft_quant(entries, peak_value):
    step_size = (peak_value + 1e-05) / LEVELS
    ratios = entries / step_size
    return step_size * (ratios - jnp.sin(2.0 * jnp.pi * ratios) / (2.0 * jnp.pi))


def body(tokens, rotation, key_weight, grad_out):
    shrink = D ** (-0.5)
    rot_low = rotation.astype(jnp.bfloat16)
    columns = lax.all_to_all(tokens, "dp", split_axis=1, concat_axis=0, tiled=True)
    rows_here = columns
    rotated = (
        lax.psum_scatter(
            jnp.dot(rows_here, rot_low, preferred_element_type=jnp.float32),
            "dp",
            scatter_dimension=0,
            tiled=True,
        )
        * shrink
    )
    token_peak = lax.pmax(jnp.max(jnp.abs(rotated), axis=1, keepdims=True), "mp")
    quant_act = soft_quant(rotated, token_peak).astype(jnp.bfloat16)
    weight_rows = lax.all_gather(key_weight, "mp", axis=1, tiled=True)
    weight_local = lax.dot_general(
        weight_rows, rot_low, CONTRACT_ROWS, preferred_element_type=jnp.float32
    )
    weight_whole = lax.psum(weight_local, "dp") * shrink
    whole_peak = lax.pmax(jnp.max(jnp.abs(weight_whole), axis=1, keepdims=True), "mp")
    quant_weight = soft_quant(weight_whole, whole_peak).astype(jnp.bfloat16)
    partial_out = lax.dot_general(
        quant_act, quant_weight, CONTRACT_COLUMNS, preferred_element_type=jnp.float32
    )
    projected = lax.psum_scatter(partial_out, "mp", scatter_dimension=1, tiled=True).astype(
        jnp.bfloat16
    )
    upstream = lax.all_gather(grad_out, "mp", axis=1, tiled=True)
    grad_act = jnp.dot(upstream, quant_weight, preferred_element_type=jnp.float32).astype(
        jnp.bfloat16
    )
    rows_here = columns
    token_grad = lax.dot_general(
        rows_here,
        lax.all_gather(grad_act, "dp", axis=0, tiled=True),
        CONTRACT_ROWS,
        preferred_element_type=jnp.float32,
    )
    grad_share = lax.psum_scatter(
        lax.dot_general(upstream, quant_act, CONTRACT_ROWS, preferred_element_type=jnp.float32),
        "dp",
        scatter_dimension=0,
        tiled=True,
    ).astype(jnp.bfloat16)
    grad_weight = lax.all_gather(grad_share, "dp", axis=0, tiled=True)
    gradient = (
        token_grad + jnp.dot(weight_rows, grad_weight, preferred_element_type=jnp.float32)
    ) * shrink
    stride = D // PANEL
    panel = rotation[:, ::stride]

    def apply_tangent(block):
        block_rows = lax.all_gather(block, "mp", axis=1, tiled=True)
        left_part = lax.dot_general(
            rotation,
            block_rows,
            CONTRACT_ROWS,
            precision=HIGHEST_PRECISION,
            preferred_element_type=jnp.float32,
        )
        right_part = lax.dot_general(
            gradient,
            block_rows,
            CONTRACT_ROWS,
            precision=HIGHEST_PRECISION,
            preferred_element_type=jnp.float32,
        )
        left_sum, right_sum = (
            lax.psum(left_part.astype(jnp.bfloat16), "dp").astype(jnp.float32),
            lax.psum(right_part.astype(jnp.bfloat16), "dp").astype(jnp.float32),
        )
        image_part = jnp.dot(gradient, left_sum, precision=HIGHEST_PRECISION) - jnp.dot(
            rotation, right_sum, precision=HIGHEST_PRECISION
        )
        return lax.psum_scatter(image_part, "mp", scatter_dimension=1, tiled=True)

    image = apply_tangent(panel)
    norm_sums = lax.psum((jnp.sum(panel * panel), jnp.sum(image * image)), ("dp", "mp"))
    alpha = STEP_GAIN * jnp.sqrt(norm_sums[0] / (norm_sums[1] + 1e-06))
    updated = panel - alpha * image
    for iteration in range(ITERS):
        updated = panel - 0.5 * alpha * (image + apply_tangent(updated))
    return (projected, updated)


def solution(mesh):
    placed = (P("dp", None), P("dp", "mp"), P("dp", "mp"), P("dp", "mp"))
    return jax.shard_map(
        body, mesh=mesh, in_specs=placed, out_specs=(P("dp", "mp"), P("dp", "mp")), check_vma=False
    )
```

profile of v0, /device:TPU:8, one launch (start us, length us, event | category | flops | bytes accessed | tf_op | source)
XLA Modules:
  0.0 1587.1 jit_solution(16539387174060462615)
XLA Ops:
  7.2 4.2 copy.15
  11.4 11.7 all-to-all-start
  23.1 12.9 all_gather.21
  36.9 2.7 fusion.7
  39.7 40.9 %all-to-all-done = bf16[128,32,256]{0,2,1:T(8,128)(2,1)S(1)} async-done(((bf16[128,32,256]{0,2,1:T(8,128)(2,1)}), bf16[128,32,256]{0,2,1:T(8,128)(2,1)S(1)}, u32[]{:S(2)}, u32[]{:S(2)}) %all-to-all-start) | async-done | bytes 2097184 | tf_op jit(solution)/shard_map/all_to_all | solution.py:27
  81.9 3.3 copy.16
  85.2 8.1 fusion.9
  94.1 12.3 all_gather.22
  106.4 111.9 %all-reduce.10.cloned.1.call-done = f32[1024,1024]{1,0:T(8,128)} async-done(((f32[1024,1024]{1,0:T(8,128)}), f32[1024,1024]{1,0:T(8,128)}) %all-reduce.10.cloned.1.call-update) | async-done | bytes 4194320 | tf_op jit(solution)/shard_map/psum | solution.py:44
  218.3 2.7 abs_reduce_fusion
  221.0 244.2 %reduce-scatter.9.cloned.1.call-done = f32[128,1024]{1,0:T(8,128)} async-done(((f32[4096,1024]{1,0:T(8,128)}), f32[128,1024]{1,0:T(8,128)}) %reduce-scatter.9.cloned.1.call-update) | async-done | bytes 524304 | tf_op jit(solution)/shard_map/reduce_scatter | solution.py:30
  466.4 12.7 all-reduce.1
  479.0 5.5 convolution_bitcast_fusion
  484.5 5.4 copy.19
  490.0 16.4 %multiply_convert_fusion = bf16[1024,1024]{1,0:T(8,128)(2,1)S(1)} fusion(f32[1024,1024]{1,0:T(8,128)} %all-reduce.10.cloned.1.call-done, f32[1024]{0:T(1024)S(1)} %bitcast.68), kind=kLoop, calls=%fused_computation | loop fusion | flops 7340032 | bytes 6295552 | tf_op jit(solution)/shard_map/convert_element_type | solution.py:46
  509.3 198.3 %reduce-scatter.19.cloned.1.call-done = f32[32,1024]{1,0:T(8,128)} async-done(((f32[1024,1024]{1,0:T(8,128)}), f32[32,1024]{1,0:T(8,128)}) %reduce-scatter.19.cloned.1.call-update) | async-done | bytes 131088 | tf_op jit(solution)/shard_map/reduce_scatter | solution.py:64
  710.3 13.1 all_gather.25
  725.9 85.6 %all-gather.3.cloned.1.call-done = bf16[4096,1024]{0,1:T(8,128)(2,1)} async-done(((bf16[128,1024]{0,1:T(8,128)(2,1)}), bf16[4096,1024]{0,1:T(8,128)(2,1)}) %all-gather.3.cloned.1.call-update) | async-done | bytes 8388624 | tf_op jit(solution)/shard_map/all_gather | solution.py:60
  811.5 6.7 fusion.12
  818.2 71.5 %all-gather.5.cloned.1.call-done = bf16[1024,1024]{1,0:T(8,128)(2,1)} async-done(((bf16[32,1024]{1,0:T(8,128)(2,1)}), bf16[1024,1024]{1,0:T(8,128)(2,1)}) %all-gather.5.cloned.1.call-update) | async-done | bytes 2097168 | tf_op jit(solution)/shard_map/all_gather | solution.py:70
  889.7 2.8 fusion
  894.3 144.9 %all-reduce.16.cloned.1.call-done = (bf16[1024,128]{1,0:T(8,128)(2,1)}, bf16[1024,128]{1,0:T(8,128)(2,1)}) async-done(((bf16[1024,128]{1,0:T(8,128)(2,1)}, bf16[1024,128]{1,0:T(8,128)(2,1)}), (bf16[1024,128]{1,0:T(8,128)(2,1)}, bf16[1024,128]{1,0:T(8,128)(2,1)})) %all-reduce.16.cloned.1.call-update) | async-done | bytes 524304 | tf_op jit(solution)/shard_map/psum | solution.py:94
  1043.6 30.4 %reduce-scatter.13.cloned.1.call-done = f32[256,16]{0,1:T(8,128)} async-done(((f32[256,128]{0,1:T(8,128)}), f32[256,16]{0,1:T(8,128)}) %reduce-scatter.13.cloned.1.call-update) | async-done | bytes 16400 | tf_op jit(solution)/shard_map/reduce_scatter | solution.py:100
  1075.5 74.0 %all-reduce = (f32[]{:T(128)}, f32[]{:T(128)}) all-reduce(f32[]{:T(128)} %multiply_reduce_fusion.1, f32[]{:T(128)} %multiply_reduce_fusion), channel_id=1, replica_groups=mesh['dp'=32,'mp'=8] {'dp','mp'}, use_global_device_ids=true, to_apply=%region_8.0 | all-reduce | flops 2 | bytes 16 | tf_op jit(solution)/shard_map/psum | solution.py:103
  1151.6 12.7 all_gather.26
  1167.5 145.1 %all-reduce.14.cloned.1.call-done = (bf16[1024,128]{0,1:T(8,128)(2,1)}, bf16[1024,128]{1,0:T(8,128)(2,1)}) async-done(((bf16[1024,128]{0,1:T(8,128)(2,1)}, bf16[1024,128]{1,0:T(8,128)(2,1)}), (bf16[1024,128]{0,1:T(8,128)(2,1)}, bf16[1024,128]{1,0:T(8,128)(2,1)})) %all-reduce.14.cloned.1.call-update) | async-done | bytes 524304 | tf_op jit(solution)/shard_map/psum | solution.py:94
  1316.5 31.0 %reduce-scatter.15.cloned.1.call-done = f32[256,16]{0,1:T(8,128)} async-done(((f32[256,128]{0,1:T(8,128)}), f32[256,16]{0,1:T(8,128)}) %reduce-scatter.15.cloned.1.call-update) | async-done | bytes 16400 | tf_op jit(solution)/shard_map/reduce_scatter | solution.py:100
  1348.2 13.0 all_gather.27
  1364.4 4.7 fusion.11
  1369.2 141.4 %all-reduce.12.cloned.1.call-done = (bf16[1024,128]{0,1:T(8,128)(2,1)}, bf16[1024,128]{1,0:T(8,128)(2,1)}) async-done(((bf16[1024,128]{0,1:T(8,128)(2,1)}, bf16[1024,128]{1,0:T(8,128)(2,1)}), (bf16[1024,128]{0,1:T(8,128)(2,1)}, bf16[1024,128]{1,0:T(8,128)(2,1)})) %all-reduce.12.cloned.1.call-update) | async-done | bytes 524304 | tf_op jit(solution)/shard_map/psum | solution.py:94
  1514.4 30.5 %reduce-scatter.11.cloned.1.call-done = f32[128,128]{1,0:T(8,128)} async-done(((f32[128,1024]{1,0:T(8,128)}), f32[128,128]{1,0:T(8,128)}) %reduce-scatter.11.cloned.1.call-update) | async-done | bytes 65552 | tf_op jit(solution)/shard_map/reduce_scatter | solution.py:50
  1546.3 32.7 %reduce-scatter.17.cloned.1.call-done = f32[256,16]{0,1:T(8,128)} async-done(((f32[256,128]{0,1:T(8,128)}), f32[256,16]{0,1:T(8,128)}) %reduce-scatter.17.cloned.1.call-update) | async-done | bytes 16400 | tf_op jit(solution)/shard_map/reduce_scatter | solution.py:100
  (65 shorter events, 38.2 us)
Async XLA Ops:
  7.2 16.0 %copy-start.6 = (bf16[256,128]{1,0:T(8,128)(2,1)S(1)}, bf16[256,128]{1,0:T(8,128)(2,1)}, u32[]{:S(2)}) copy-start(bf16[256,128]{1,0:T(8,128)(2,1)} %param.6) | copy-start | bytes 196612
  7.2 29.7 %copy-start = (f32[256,1024]{1,0:T(8,128)S(1)}, f32[256,1024]{1,0:T(8,128)}, u32[]{:S(2)}) copy-start(f32[256,1024]{1,0:T(8,128)} %param.5) | copy-start | bytes 3145732
  11.4 69.2 %all-to-all-start = ((bf16[128,32,256]{0,2,1:T(8,128)(2,1)}), bf16[128,32,256]{0,2,1:T(8,128)(2,1)S(1)}, u32[]{:S(2)}, u32[]{:S(2)}) async-start(bf16[128,32,256]{0,2,1:T(8,128)(2,1)} %bitcast.66), calls=%async_computation | async-start | bytes 4194304 | tf_op jit(solution)/shard_map/all_to_all | solution.py:27
  23.1 195.2 %all-reduce.10.cloned.1.call-start = ((), (), s32[]{:S(2)}) async-start(), calls=%async_computation.8 | async-start | bytes 8388608 | tf_op jit(solution)/shard_map/psum | solution.py:44
  36.0 0.8 copy-start.3
  39.6 425.6 %reduce-scatter.9.cloned.1.call-start = ((), (), s32[]{:S(2)}) async-start(), calls=%async_computation.7 | async-start | bytes 17301504 | tf_op jit(solution)/shard_map/reduce_scatter | solution.py:30
  80.6 1.4 copy-start.2
  93.4 0.8 copy-start.7
  93.4 614.3 %reduce-scatter.19.cloned.1.call-start = ((), (), s32[]{:S(2)}) async-start(), calls=%async_computation.15 | async-start | bytes 4325376 | tf_op jit(solution)/shard_map/reduce_scatter | solution.py:64
  489.9 321.6 %all-gather.3.cloned.1.call-start = ((), (), s32[]{:S(2)}) async-start(), calls=%async_computation.10 | async-start | bytes 8650752 | tf_op jit(solution)/shard_map/all_gather | solution.py:60
  506.4 1.3 copy-start.1
  509.3 380.4 %all-gather.5.cloned.1.call-start = ((), (), s32[]{:S(2)}) async-start(), calls=%async_computation.11 | async-start | bytes 2162688 | tf_op jit(solution)/shard_map/all_gather | solution.py:70
  709.2 329.9 %all-reduce.16.cloned.1.call-start = ((), (), s32[]{:S(2)}) async-start(), calls=%async_computation.18 | async-start | bytes 1048576 | tf_op jit(solution)/shard_map/psum | solution.py:94
  894.2 179.9 %reduce-scatter.13.cloned.1.call-start = ((), (), s32[]{:S(2)}) async-start(), calls=%async_computation.12 | async-start | bytes 147456 | tf_op jit(solution)/shard_map/reduce_scatter | solution.py:100
  1043.0 269.7 %all-reduce.14.cloned.1.call-start = ((), (), s32[]{:S(2)}) async-start(), calls=%async_computation.17 | async-start | bytes 1048576 | tf_op jit(solution)/shard_map/psum | solution.py:94
  1074.1 273.4 %copy-start.5 = (f32[256,16]{0,1:T(8,128)S(1)}, f32[256,16]{0,1:T(8,128)}, u32[]{:S(2)}) copy-start(f32[256,16]{0,1:T(8,128)} %reduce-scatter.13.cloned.1.call-done) | copy-start | bytes 49156
  1166.0 198.4 %copy-start.4 = (f32[128,1024]{1,0:T(8,128)S(1)}, f32[128,1024]{1,0:T(8,128)}, u32[]{:S(2)}) copy-start(f32[128,1024]{1,0:T(8,128)} %reduce-scatter.9.cloned.1.call-done) | copy-start | bytes 1572868
  1167.5 180.0 %reduce-scatter.15.cloned.1.call-start = ((), (), s32[]{:S(2)}) async-start(), calls=%async_computation.13 | async-start | bytes 147456 | tf_op jit(solution)/shard_map/reduce_scatter | solution.py:100
  1316.4 194.2 %all-reduce.12.cloned.1.call-start = ((), (), s32[]{:S(2)}) async-start(), calls=%async_computation.16 | async-start | bytes 1048576 | tf_op jit(solution)/shard_map/psum | solution.py:94
  1364.3 180.5 %reduce-scatter.11.cloned.1.call-start = ((), (), s32[]{:S(2)}) async-start(), calls=%async_computation.9 | async-start | bytes 589824 | tf_op jit(solution)/shard_map/reduce_scatter | solution.py:50
  1369.2 209.8 %reduce-scatter.17.cloned.1.call-start = ((), (), s32[]{:S(2)}) async-start(), calls=%async_computation.14 | async-start | bytes 147456 | tf_op jit(solution)/shard_map/reduce_scatter | solution.py:100
Sparse Core Ops, SparseCore 0:
  39.7 178.4 all-reduce.9
  222.9 242.2 reduce-scatter.8
  490.1 217.5 reduce-scatter.18
  710.0 101.4 all-gather.2
  813.9 75.7 all-gather.4
  894.3 144.7 all-reduce.15
  1043.1 30.9 reduce-scatter.12
  1167.6 145.0 all-reduce.13
  1316.6 30.8 reduce-scatter.14
  1364.5 146.0 all-reduce.11
  1513.3 31.5 reduce-scatter.10
  1547.2 31.7 reduce-scatter.16
where the time goes:
time: 1590 us
  waiting for transfers between devices  1310 us (82%)
  blocking collectives  151 us (9%)
  matrix products  53.9 us (3%)
  other arithmetic  28.1 us (2%)
  local copies, waits for them, and re-layouts  17.9 us (1%)
    psum x3, waiting for transfers between devices, apply_tangent(): lax.psum(left_part.astype(jnp.bfloat16), 'dp').astype(jnp.float32)  431 us
    reduce_scatter x1, waiting for transfers between devices, body(): lax.psum_scatter(jnp.dot(rows_here, rot_low, preferred_element_type=jnp.f...  244 us
    reduce_scatter x1, waiting for transfers between devices, body(): lax.psum_scatter(lax.dot_general(upstream, quant_act, CONTRACT_ROWS, pref...  198 us
    psum x1, waiting for transfers between devices, body(): weight_whole = lax.psum(weight_local, 'dp') * shrink  112 us
    reduce_scatter x3, waiting for transfers between devices, apply_tangent(): return lax.psum_scatter(image_part, 'mp', scatter_dimension=1, tiled=True)  94.1 us
    all_gather x1, waiting for transfers between devices, body(): lax.all_gather(grad_act, 'dp', axis=0, tiled=True)  85.6 us
    psum x1, blocking collectives, body(): lax.psum((jnp.sum(panel * panel), jnp.sum(image * image)), ('dp', 'mp'))  74 us
    all_gather x1, waiting for transfers between devices, body(): grad_weight = lax.all_gather(grad_share, 'dp', axis=0, tiled=True)  71.5 us
  transfers between devices with their start and end apart: 13, of which 13 were waited for; matrix products, arithmetic and copies ran while one was open for 4% of the time, Pallas kernels for 0%

commit v1 on v0

v1 whole, which is shorter than its diff:
```python
import jax
import jax.numpy as jnp
from jax import lax
from jax.sharding import Mesh, PartitionSpec as P

D = 8192
F = 1024
PANEL = 128
STEP_GAIN = 0.8
LEVELS = 7.0

SIZE = {"y": 4, "z": 8, "x": 4, "c": 2}
MP = ("x", "c")
NMP = 8
KA, GA = "y", "z"
NK, NG = SIZE[KA], SIZE[GA]
ROWS = NG * 256
TOKS = NK * 128
COLS = 1024 // NK
SUB = 128 // NG
UNITS = NMP * SUB

LAST = (((1,), (1,)), ((), ()))
bf16, f32 = jnp.bfloat16, jnp.float32


def soft_quant(entries, peak_value):
    step_size = (peak_value + 1e-05) / LEVELS
    ratios = entries / step_size
    return step_size * (ratios - jnp.sin(2.0 * jnp.pi * ratios) / (2.0 * jnp.pi))


def dot(a, b):
    return jnp.dot(a, b, preferred_element_type=f32)


def dot_last(a, b):
    return lax.dot_general(a, b, LAST, preferred_element_type=f32)


def gather(block, axis):
    return lax.all_gather(block, axis, axis=0, tiled=False)


def exchange(blocks, axis):
    return lax.all_to_all(blocks, axis, split_axis=0, concat_axis=0, tiled=True)


def send_all(block, axis):
    n = SIZE[axis]
    return [
        lax.ppermute(block, axis, [(s, (s + k) % n) for s in range(n)]) for k in range(1, n)
    ]


def sum_all(block, axis):
    low = block.astype(bf16)
    total = low.astype(f32)
    for other in send_all(low, axis):
        total = total + other.astype(f32)
    return total


def sum_exact(values, axis):
    total = values
    for other in send_all(values, axis):
        total = total + other
    return total


def sum_with(block, scalars, axis):
    terms = []
    for value in scalars:
        for _ in range(3):
            term = lax.reduce_precision(value, 8, 7)
            terms.append(term)
            value = value - term
    rest = jnp.zeros((16 - len(terms),), f32)
    extra = jnp.broadcast_to(jnp.concatenate([jnp.stack(terms), rest])[:, None], (16, 128))
    total = sum_all(jnp.concatenate([block, extra], 1), axis)
    extra = total[:, -128:]
    sums = [extra[3 * k, 0] + extra[3 * k + 1, 0] + extra[3 * k + 2, 0] for k in range(len(scalars))]
    return total[:, :-128], sums


def body(tokens, rotation, key_weight, grad_out):
    shrink = D ** (-0.5)
    mp = lax.axis_index(MP)
    g = lax.axis_index(GA)

    rot_low = rotation.astype(bf16)
    rot = gather(rot_low, GA).reshape(ROWS, 1024)

    part = lax.dynamic_slice(tokens, (16 * mp, 0), (16, D)).reshape(16, 4, 8, 256)
    part = part.transpose((2, 0, 1, 3) if KA == "z" else (1, 0, 2, 3)).reshape(NK, 16, ROWS)
    tok = gather(exchange(part, KA), MP).reshape(TOKS, ROWS)

    wt = exchange(key_weight.T.reshape(NG, SUB, 256), GA)
    wt = wt.transpose(1, 0, 2).reshape(SUB, ROWS)
    wt = gather(wt, MP).reshape(UNITS, ROWS)

    product = dot(jnp.concatenate([tok, wt], 0), rot).astype(bf16)
    product = product.reshape(TOKS + UNITS, NK, COLS).transpose(1, 0, 2)
    rotated = jnp.sum(exchange(product, KA).astype(f32), axis=0) * shrink
    peak = jnp.max(jnp.abs(rotated), axis=1)
    peak = lax.pmax(lax.pmax(peak, MP), KA)[:, None]
    quant = soft_quant(rotated, peak).astype(bf16)
    quant_act, quant_weight = quant[:TOKS], quant[TOKS:]

    up = gather(grad_out.T, KA)
    up = up.reshape(NK, 128, NMP, 16).transpose(1, 2, 0, 3).reshape(128, TOKS)
    up_all = gather(up, MP).reshape(NMP, NG, SUB, TOKS).transpose(1, 0, 2, 3).reshape(F, TOKS)

    ct = dot(up, tok).astype(bf16).reshape(NG, SUB, ROWS)
    ct = jnp.sum(exchange(ct, GA).astype(f32), axis=0).astype(bf16)
    ct = gather(ct, MP).reshape(UNITS, ROWS)

    gw = dot(up_all, quant_act).astype(bf16).reshape(NG, UNITS, COLS)
    gw = jnp.sum(exchange(gw, GA).astype(f32), axis=0).astype(bf16)
    yk = jnp.concatenate([quant_weight, gw], 0)
    ymat = gather(yk, KA).transpose(1, 0, 2).reshape(2 * UNITS, 1024)
    zt = (dot_last(ymat, rot) * shrink).astype(bf16)
    zt = exchange(zt.reshape(NMP, 2 * UNITS // NMP, ROWS), MP)
    zt = jnp.sum(zt.astype(f32), axis=0).astype(bf16)
    zt = gather(zt, MP).reshape(2 * UNITS, ROWS)

    ut = jnp.concatenate([ct, wt, zt], 0)

    qw_all = gather(quant_weight, GA).reshape(NG, NMP, SUB, COLS).transpose(1, 0, 2, 3)
    projected = dot_last(quant_act, qw_all.reshape(F, COLS)).astype(bf16)
    projected = lax.psum_scatter(projected, MP, scatter_dimension=1, tiled=True)
    projected = projected.reshape(NMP, NK, 16, 128).transpose(1, 0, 2, 3).reshape(TOKS, 128)
    projected = lax.psum_scatter(projected, KA, scatter_dimension=0, tiled=True)

    own = rotation[:, :: D // PANEL].T
    panel = gather(own, GA).transpose(1, 0, 2).reshape(16, ROWS)

    def inner(block):
        return dot_last(block.astype(bf16), ut)

    def outer(v):
        v = v.astype(bf16)
        v = jnp.concatenate([v[:, 2 * UNITS :], -v[:, : 2 * UNITS]], 1)
        return sum_all(dot(v, ut), GA)

    w1 = outer(sum_all(inner(panel), KA))
    v, sums = sum_with(inner(w1), (jnp.sum(panel * panel), jnp.sum(w1 * w1)), KA)
    unit = lax.rsqrt(sums[1] + 1e-06)
    w2 = outer(v * unit)
    totals = jnp.broadcast_to(jnp.stack(sums)[:, None], (2, 128))
    for axis in MP:
        totals = sum_exact(totals, axis)
    alpha = STEP_GAIN * jnp.sqrt(totals[0, 0] / (totals[1, 0] + 1e-06))
    ratio = STEP_GAIN * jnp.sqrt(totals[0, 0] * ((sums[1] + 1e-06) / (totals[1, 0] + 1e-06)))
    w3 = outer(sum_all(inner(w2), KA) * unit)
    step = alpha * (w1 - ratio * (0.5 * w2 - 0.25 * ratio * w3))
    step = lax.dynamic_slice(step, (0, g * 256), (16, 256))
    return projected, (own - step).T


def solution(mesh):
    grid = Mesh(mesh.devices.reshape(4, 8, 4, 2), ("y", "z", "x", "c"))
    dp = ("y", "z")
    placed = (P(dp, None), P(dp, MP), P(dp, MP), P(dp, MP))
    return jax.shard_map(
        body, mesh=grid, in_specs=placed, out_specs=(P(dp, MP), P(dp, MP)), check_vma=False
    )
```

time: 1590 us -> 438 us (0.28)
  waiting for transfers between devices: 1310 us -> 91.4 us
  starting transfers between devices: 12.4 us -> 96.8 us
  matrix products: 53.9 us -> 22.4 us
  other arithmetic: 28.1 us -> 12.2 us
    reduce_scatter x6 -> x1, waiting for transfers between devices: 567 us -> 0.01 us  [body(): projected = lax.psum_scatter(projected, KA, scatter_dimension=0, tiled=True)]
    psum x4 -> x0, waiting for transfers between devices: 543 us -> none  [the longest x3 431 us: apply_tangent(): lax.psum(left_part.astype(jnp.bfloat16), 'dp').astype(jnp.float32)]
    all_gather x2 -> x4, waiting for transfers between devices: 157 us -> 66.2 us  [gather(): return lax.all_gather(block, axis, axis=0, tiled=False)]
    psum x1 -> x0, blocking collectives: 74 us -> none  [body(): lax.psum((jnp.sum(panel * panel), jnp.sum(image * image)), ('dp', 'mp'))]
    ppermute x0 -> x34, starting transfers between devices: none -> 74 us  [send_all(): lax.ppermute(block, axis, [(s, (s + k) % n) for s in range(n)])]
    all_gather x5 -> x6, blocking collectives: 63.9 us -> 106 us  [gather(): return lax.all_gather(block, axis, axis=0, tiled=False)]
    dot_general x19 -> x11, matrix products: 53.9 us -> 22.4 us  [the longest x6 13.7 us: dot(): return jnp.dot(a, b, preferred_element_type=f32)]
    all_to_all x0 -> x2, blocking collectives: none -> 29 us  [exchange(): return lax.all_to_all(blocks, axis, split_axis=0, concat_axis=0, tiled=True)]
  transfers between devices with their start and end apart: 13 -> 44, of which waited for: 13 -> 12; matrix products, arithmetic and copies ran while one was open for 4% -> 7% of each run, Pallas kernels for 0% -> 0%
where the time goes in v1:
time: 438 us; the launch traced here: 432 us
  blocking collectives  158 us (36%)
  starting transfers between devices  96.8 us (22%)
  waiting for transfers between devices  91.4 us (21%)
  between operations  28.7 us (7%)
  local copies, waits for them, and re-layouts  22.9 us (5%)
  matrix products  22.4 us (5%)
  other arithmetic  12.2 us (3%)
    all_gather x6, blocking collectives, gather(): return lax.all_gather(block, axis, axis=0, tiled=False)  106 us
    ppermute x34, starting transfers between devices, send_all(): lax.ppermute(block, axis, [(s, (s + k) % n) for s in range(n)])  74 us
    all_gather x4, waiting for transfers between devices, gather(): return lax.all_gather(block, axis, axis=0, tiled=False)  66.2 us
    all_to_all x2, blocking collectives, exchange(): return lax.all_to_all(blocks, axis, split_axis=0, concat_axis=0, tiled=True)  29 us
    pmax x2, blocking collectives, body(): peak = lax.pmax(lax.pmax(peak, MP), KA)[:, None]  22.8 us
    all_to_all x4, starting transfers between devices, exchange(): return lax.all_to_all(blocks, axis, split_axis=0, concat_axis=0, tiled=True)  22.6 us
    all_to_all x4, waiting for transfers between devices, exchange(): return lax.all_to_all(blocks, axis, split_axis=0, concat_axis=0, tiled=True)  14.7 us
    dot_general x6, matrix products, dot(): return jnp.dot(a, b, preferred_element_type=f32)  13.7 us
  transfers between devices with their start and end apart: 44, of which 12 were waited for; matrix products, arithmetic and copies ran while one was open for 7% of the time, Pallas kernels for 0%

profile of v1, /device:TPU:8, one launch (start us, length us, event | category | flops | bytes accessed | tf_op | source)
XLA Modules:
  0.0 432.0 jit_solution(7304751792521865179)
XLA Ops:
  10.9 10.5 %all_to_all.30 = bf16[4,16,2048]{2,1,0:T(8,128)(2,1)} all-to-all(bf16[4,16,2048]{2,1,0:T(8,128)(2,1)S(1)} %copy.44), channel_id=1, replica_groups=mesh['y'=4,'z'=8,'x'=4,'c'=2] {'y'}, dimensions={0} | all-to-all | bytes 524288 | tf_op jit(solution)/shard_map/all_to_all | solution.py:46
  23.0 8.0 %all-to-all-start.1 = ((bf16[8,16,256]{2,1,0:T(8,128)(2,1)}), bf16[8,16,256]{2,1,0:T(8,128)(2,1)S(1)}, u32[]{:S(2)}, u32[]{:S(2)}) async-start(bf16[8,16,256]{2,1,0:T(8,128)(2,1)} %bitcast.3), calls=%async_computation.1 | async-start | bytes 131072 | tf_op jit(solution)/shard_map/all_to_all | solution.py:46
  31.1 10.4 %all-gather.3 = bf16[512,128]{0,1:T(8,128)(2,1)S(1)} all-gather(bf16[128,128]{0,1:T(8,128)(2,1)S(1)} %bitcast.123), channel_id=5, replica_groups=mesh['y'=4,'z'=8,'x'=4,'c'=2] {'y'}, dimensions={0}, use_global_device_ids=true | all-gather | bytes 163840 | tf_op jit(solution)/shard_map/all_gather | solution.py:42
  42.5 13.8 %all_gather.56 = bf16[8,16,2048]{2,1,0:T(8,128)(2,1)S(1)} all-gather(bf16[1,16,2048]{2,1,0:T(8,128)(2,1)S(1)} %all_gather_reshape.6), channel_id=1, replica_groups=mesh['y'=4,'z'=8,'x'=4,'c'=2] {'x','c'}, dimensions={0}, use_global_device_ids=true | all-gather | bytes 589824 | tf_op jit(solution)/shard_map/all_gather | solution.py:42
  56.3 51.6 %all-gather.17.cloned.1.call-done = bf16[2048,1024]{1,0:T(8,128)(2,1)} async-done(((bf16[256,1024]{1,0:T(8,128)(2,1)}), bf16[2048,1024]{1,0:T(8,128)(2,1)}) %all-gather.17.cloned.1.call-update) | async-done | bytes 4194320 | tf_op jit(solution)/shard_map/all_gather | solution.py:42
  108.0 5.7 %fusion.6 = bf16[640,1024]{1,0:T(8,128)(2,1)S(1)} fusion(bf16[2048,1024]{1,0:T(8,128)(2,1)} %all-gather.17.cloned.1.call-done, bf16[128,2048]{1,0:T(8,128)(2,1)S(1)} %bitcast.107, bf16[512,2048]{1,0:T(8,128)(2,1)} %bitcast.95), kind=kOutput, calls=%fused_computation.13 | convolution fusion | flops 2690252800 | bytes 8126464 | tf_op jit(solution)/shard_map/dot_general | solution.py:34
  114.9 4.8 %all-to-all-start.2 = ((bf16[4,640,256]{2,1,0:T(8,128)(2,1)}), bf16[4,640,256]{2,1,0:T(8,128)(2,1)}, u32[]{:S(2)}, u32[]{:S(2)}) async-start(bf16[4,640,256]{2,1,0:T(8,128)(2,1)} %bitcast.93), calls=%async_computation.2 | async-start | bytes 2621440 | tf_op jit(solution)/shard_map/all_to_all | solution.py:46
  119.7 14.6 %all-gather.13.cloned.1.call-done = bf16[8,128,512]{2,1,0:T(8,128)(2,1)} async-done(((bf16[1,128,512]{2,1,0:T(8,128)(2,1)}), bf16[8,128,512]{2,1,0:T(8,128)(2,1)}) %all-gather.13.cloned.1.call-update) | async-done | bytes 1048592 | tf_op jit(solution)/shard_map/all_gather | solution.py:42
  138.4 13.6 %pmax.14 = f32[640]{0:T(1024)S(1)} all-reduce(f32[640]{0:T(1024)S(1)} %abs_reduce_fusion), channel_id=1, replica_groups=mesh['y'=4,'z'=8,'x'=4,'c'=2] {'x','c'}, use_global_device_ids=true, to_apply=%region_2.0 | all-reduce | flops 640 | bytes 5120 | tf_op jit(solution)/shard_map/pmax | solution.py:106
  152.0 9.2 %pmax.15 = f32[640]{0:T(1024)S(1)} all-reduce(f32[640]{0:T(1024)S(1)} %pmax.14), channel_id=1, replica_groups=mesh['y'=4,'z'=8,'x'=4,'c'=2] {'y'}, use_global_device_ids=true, to_apply=%region_3.0 | all-reduce | flops 640 | bytes 5120 | tf_op jit(solution)/shard_map/pmax | solution.py:106
  166.4 6.1 %all-to-all-start.4 = ((bf16[8,128,256]{1,2,0:T(8,128)(2,1)}), bf16[8,128,256]{1,2,0:T(8,128)(2,1)S(1)}, u32[]{:S(2)}, u32[]{:S(2)}) async-start(bf16[8,128,256]{1,2,0:T(8,128)(2,1)} %bitcast.94), calls=%async_computation.5 | async-start | bytes 1048576 | tf_op jit(solution)/shard_map/all_to_all | solution.py:46
  172.6 14.7 %all-to-all-done.4 = bf16[8,128,256]{1,2,0:T(8,128)(2,1)S(1)} async-done(((bf16[8,128,256]{1,2,0:T(8,128)(2,1)}), bf16[8,128,256]{1,2,0:T(8,128)(2,1)S(1)}, u32[]{:S(2)}, u32[]{:S(2)}) %all-to-all-start.4) | async-done | bytes 524320 | tf_op jit(solution)/shard_map/all_to_all | solution.py:46
  187.5 12.4 %all-gather.5 = bf16[1024,256]{1,0:T(8,128)(2,1)S(1)} all-gather(bf16[256,256]{1,0:T(8,128)(2,1)S(1)} %pad_maximum_fusion.1), channel_id=7, replica_groups=mesh['y'=4,'z'=8,'x'=4,'c'=2] {'y'}, dimensions={0}, use_global_device_ids=true | all-gather | bytes 655360 | tf_op jit(solution)/shard_map/all_gather | solution.py:42
  200.1 3.5 fusion.4
  203.6 18.5 %all_to_all.31 = bf16[8,32,2048]{2,1,0:T(8,128)(2,1)S(1)} all-to-all(bf16[8,32,2048]{2,1,0:T(8,128)(2,1)S(1)} %bitcast.105), channel_id=1, replica_groups=mesh['y'=4,'z'=8,'x'=4,'c'=2] {'x','c'}, dimensions={0} | all-to-all | bytes 2097152 | tf_op jit(solution)/shard_map/all_to_all | solution.py:46
  222.9 2.9 fusion.5
  225.8 3.6 all-to-all-start.3
  232.8 29.4 %all-gather.7 = f32[128,256]{1,0:T(8,128)S(1)} all-gather(f32[16,256]{1,0:T(8,128)S(1)} %bitcast.120), channel_id=9, replica_groups=mesh['y'=4,'z'=8,'x'=4,'c'=2] {'z'}, dimensions={0}, use_global_device_ids=true | all-gather | bytes 147456 | tf_op jit(solution)/shard_map/all_gather | solution.py:42
  264.2 13.3 %all-gather.4 = bf16[128,2048]{1,0:T(8,128)(2,1)S(1)} all-gather(bf16[16,2048]{1,0:T(8,128)(2,1)} %reduce_sum.64), channel_id=6, replica_groups=mesh['y'=4,'z'=8,'x'=4,'c'=2] {'x','c'}, dimensions={0}, use_global_device_ids=true | all-gather | bytes 589824 | tf_op jit(solution)/shard_map/all_gather | solution.py:42
  279.6 3.0 collective-permute-start
  282.6 2.7 collective-permute-start.1
  285.3 2.7 collective-permute-done.1
  292.3 2.7 collective-permute-start.4
  300.0 3.0 collective-permute-start.6
  305.3 3.8 collective-permute-start.8
  309.8 26.5 %all-gather.2 = bf16[1024,256]{1,0:T(8,128)(2,1)S(1)} all-gather(bf16[128,256]{1,0:T(8,128)(2,1)S(1)} %slice.82), channel_id=4, replica_groups=mesh['y'=4,'z'=8,'x'=4,'c'=2] {'z'}, dimensions={0}, use_global_device_ids=true | all-gather | bytes 589824 | tf_op jit(solution)/shard_map/all_gather | solution.py:42
  343.4 3.8 concatenate.29
  362.5 12.2 %collective-permute-start.18 = (bf16[16,2048]{1,0:T(8,128)(2,1)S(1)}, bf16[16,2048]{1,0:T(8,128)(2,1)S(1)}, u32[]{:S(2)}, u32[]{:S(2)}) collective-permute-start(bf16[16,2048]{1,0:T(8,128)(2,1)S(1)} %convolution_convert_fusion.1), channel_id=1, source_target_pairs={{0,16},{8,24},{16,32},{24,40},{32,48},{40,56},{48,0},{56,8},{1,17}... | collective-permute-start | bytes 196616 | tf_op jit(solution)/shard_map/ppermute | solution.py:52
  376.0 2.8 collective-permute-start.20
  378.8 3.8 collective-permute-start.21
  407.4 3.1 collective-permute-start.30
  420.2 3.0 collective-permute-done.32
  (164 shorter events, 83.5 us)
Async XLA Ops:
  7.2 49.1 %all-gather.15.cloned.1.call-start = ((), (), s32[]{:S(2)}) async-start(), calls=%async_computation.10 | async-start | bytes 2359296 | tf_op jit(solution)/shard_map/all_gather | solution.py:42
  21.3 86.6 %all-gather.17.cloned.1.call-start = ((), (), s32[]{:S(2)}) async-start(), calls=%async_computation.11 | async-start | bytes 4718592 | tf_op jit(solution)/shard_map/all_gather | solution.py:42
  23.0 19.4 %all-to-all-start.1 = ((bf16[8,16,256]{2,1,0:T(8,128)(2,1)}), bf16[8,16,256]{2,1,0:T(8,128)(2,1)S(1)}, u32[]{:S(2)}, u32[]{:S(2)}) async-start(bf16[8,16,256]{2,1,0:T(8,128)(2,1)} %bitcast.3), calls=%async_computation.1 | async-start | bytes 131072 | tf_op jit(solution)/shard_map/all_to_all | solution.py:46
  31.1 103.3 %all-gather.13.cloned.1.call-start = ((), (), s32[]{:S(2)}) async-start(), calls=%async_computation.9 | async-start | bytes 1179648 | tf_op jit(solution)/shard_map/all_gather | solution.py:42
  114.9 21.7 %all-to-all-start.2 = ((bf16[4,640,256]{2,1,0:T(8,128)(2,1)}), bf16[4,640,256]{2,1,0:T(8,128)(2,1)}, u32[]{:S(2)}, u32[]{:S(2)}) async-start(bf16[4,640,256]{2,1,0:T(8,128)(2,1)} %bitcast.93), calls=%async_computation.2 | async-start | bytes 2621440 | tf_op jit(solution)/shard_map/all_to_all | solution.py:46
  166.4 20.8 %all-to-all-start.4 = ((bf16[8,128,256]{1,2,0:T(8,128)(2,1)}), bf16[8,128,256]{1,2,0:T(8,128)(2,1)S(1)}, u32[]{:S(2)}, u32[]{:S(2)}) async-start(bf16[8,128,256]{1,2,0:T(8,128)(2,1)} %bitcast.94), calls=%async_computation.5 | async-start | bytes 1048576 | tf_op jit(solution)/shard_map/all_to_all | solution.py:46
  172.5 105.0 %all-gather.19.cloned.1.call-start = ((), (), s32[]{:S(2)}) async-start(), calls=%async_computation.12 | async-start | bytes 1179648 | tf_op jit(solution)/shard_map/all_gather | solution.py:42
  225.8 37.7 %all-to-all-start.3 = ((bf16[8,16,2048]{2,1,0:T(8,128)(2,1)}), bf16[8,16,2048]{2,1,0:T(8,128)(2,1)S(1)}, u32[]{:S(2)}, u32[]{:S(2)}) async-start(bf16[8,16,2048]{2,1,0:T(8,128)(2,1)} %bitcast.20), calls=%async_computation.4 | async-start | bytes 1048576 | tf_op jit(solution)/shard_map/all_to_all | solution.py:46
  229.5 171.8 %reduce-scatter.7.cloned.1.call-start = ((), (), s32[]{:S(2)}) async-start(), calls=%async_computation.13 | async-start | bytes 1179648
  290.1 15.3 %collective-permute-start.3 = (bf16[16,2048]{1,0:T(8,128)(2,1)}, bf16[16,2048]{1,0:T(8,128)(2,1)}, u32[]{:S(2)}, u32[]{:S(2)}) collective-permute-start(bf16[16,2048]{1,0:T(8,128)(2,1)} %convolution_convert_fusion.2), channel_id=1, source_target_pairs={{0,8},{8,16},{16,24},{24,32},{32,40},{40,48},{48,56},{56,0},{1,9},... | collective-permute-start | bytes 196616 | tf_op jit(solution)/shard_map/ppermute | solution.py:52
  292.3 16.9 %collective-permute-start.4 = (bf16[16,2048]{1,0:T(8,128)(2,1)}, bf16[16,2048]{1,0:T(8,128)(2,1)}, u32[]{:S(2)}, u32[]{:S(2)}) collective-permute-start(bf16[16,2048]{1,0:T(8,128)(2,1)} %convolution_convert_fusion.2), channel_id=1, source_target_pairs={{0,16},{8,24},{16,32},{24,40},{32,48},{40,56},{48,0},{56,8},{1,17}... | collective-permute-start | bytes 196616 | tf_op jit(solution)/shard_map/ppermute | solution.py:52
  299.1 38.0 %collective-permute-start.5 = (bf16[16,2048]{1,0:T(8,128)(2,1)}, bf16[16,2048]{1,0:T(8,128)(2,1)S(1)}, u32[]{:S(2)}, u32[]{:S(2)}) collective-permute-start(bf16[16,2048]{1,0:T(8,128)(2,1)} %convolution_convert_fusion.2), channel_id=1, source_target_pairs={{0,24},{8,32},{16,40},{24,48},{32,56},{40,0},{48,8},{56,16},{1,25}... | collective-permute-start | bytes 196616 | tf_op jit(solution)/shard_map/ppermute | solution.py:52
  300.0 37.1 %collective-permute-start.6 = (bf16[16,2048]{1,0:T(8,128)(2,1)}, bf16[16,2048]{1,0:T(8,128)(2,1)S(1)}, u32[]{:S(2)}, u32[]{:S(2)}) collective-permute-start(bf16[16,2048]{1,0:T(8,128)(2,1)} %convolution_convert_fusion.2), channel_id=1, source_target_pairs={{0,32},{8,40},{16,48},{24,56},{32,0},{40,8},{48,16},{56,24},{1,33}... | collective-permute-start | bytes 196616 | tf_op jit(solution)/shard_map/ppermute | solution.py:52
  303.0 34.1 %collective-permute-start.7 = (bf16[16,2048]{1,0:T(8,128)(2,1)}, bf16[16,2048]{1,0:T(8,128)(2,1)S(1)}, u32[]{:S(2)}, u32[]{:S(2)}) collective-permute-start(bf16[16,2048]{1,0:T(8,128)(2,1)} %convolution_convert_fusion.2), channel_id=1, source_target_pairs={{0,40},{8,48},{16,56},{24,0},{32,8},{40,16},{48,24},{56,32},{1,41}... | collective-permute-start | bytes 196616 | tf_op jit(solution)/shard_map/ppermute | solution.py:52
  305.3 31.8 %collective-permute-start.8 = (bf16[16,2048]{1,0:T(8,128)(2,1)}, bf16[16,2048]{1,0:T(8,128)(2,1)S(1)}, u32[]{:S(2)}, u32[]{:S(2)}) collective-permute-start(bf16[16,2048]{1,0:T(8,128)(2,1)} %convolution_convert_fusion.2), channel_id=1, source_target_pairs={{0,48},{8,56},{16,0},{24,8},{32,16},{40,24},{48,32},{56,40},{1,49}... | collective-permute-start | bytes 196616 | tf_op jit(solution)/shard_map/ppermute | solution.py:52
  309.2 28.0 %collective-permute-start.9 = (bf16[16,2048]{1,0:T(8,128)(2,1)}, bf16[16,2048]{1,0:T(8,128)(2,1)S(1)}, u32[]{:S(2)}, u32[]{:S(2)}) collective-permute-start(bf16[16,2048]{1,0:T(8,128)(2,1)} %convolution_convert_fusion.2), channel_id=1, source_target_pairs={{0,56},{8,0},{16,8},{24,16},{32,24},{40,32},{48,40},{56,48},{1,57}... | collective-permute-start | bytes 196616 | tf_op jit(solution)/shard_map/ppermute | solution.py:52
  349.3 6.3 %collective-permute-start.10 = (bf16[16,640]{1,0:T(8,128)(2,1)S(1)}, bf16[16,640]{1,0:T(8,128)(2,1)S(1)}, u32[]{:S(2)}, u32[]{:S(2)}) collective-permute-start(bf16[16,640]{1,0:T(8,128)(2,1)S(1)} %pad_maximum_fusion.2), channel_id=1, source_target_pairs={{0,64},{64,128},{128,192},{192,0},{1,65},{65,129},{129,193},{193,1... | collective-permute-start | bytes 61448 | tf_op jit(solution)/shard_map/ppermute | solution.py:52
  349.3 6.2 %collective-permute-start.11 = (bf16[16,640]{1,0:T(8,128)(2,1)S(1)}, bf16[16,640]{1,0:T(8,128)(2,1)}, u32[]{:S(2)}, u32[]{:S(2)}) collective-permute-start(bf16[16,640]{1,0:T(8,128)(2,1)S(1)} %pad_maximum_fusion.2), channel_id=1, source_target_pairs={{0,128},{64,192},{128,0},{192,64},{1,129},{65,193},{129,1},{193,65... | collective-permute-start | bytes 61448 | tf_op jit(solution)/shard_map/ppermute | solution.py:52
  355.5 69.4 %reduce-scatter.5.cloned.1.call-start = ((), (), s32[]{:S(2)}) async-start(), calls=%async_computation.8 | async-start | bytes 163840 | tf_op jit(solution)/shard_map/reduce_scatter | solution.py:133
  361.1 21.5 %collective-permute-start.17 = (bf16[16,2048]{1,0:T(8,128)(2,1)S(1)}, bf16[16,2048]{1,0:T(8,128)(2,1)S(1)}, u32[]{:S(2)}, u32[]{:S(2)}) collective-permute-start(bf16[16,2048]{1,0:T(8,128)(2,1)S(1)} %convolution_convert_fusion.1), channel_id=1, source_target_pairs={{0,8},{8,16},{16,24},{24,32},{32,40},{40,48},{48,56},{56,0},{1,9},... | collective-permute-start | bytes 196616 | tf_op jit(solution)/shard_map/ppermute | solution.py:52
  362.5 22.3 %collective-permute-start.18 = (bf16[16,2048]{1,0:T(8,128)(2,1)S(1)}, bf16[16,2048]{1,0:T(8,128)(2,1)S(1)}, u32[]{:S(2)}, u32[]{:S(2)}) collective-permute-start(bf16[16,2048]{1,0:T(8,128)(2,1)S(1)} %convolution_convert_fusion.1), channel_id=1, source_target_pairs={{0,16},{8,24},{16,32},{24,40},{32,48},{40,56},{48,0},{56,8},{1,17}... | collective-permute-start | bytes 196616 | tf_op jit(solution)/shard_map/ppermute | solution.py:52
  374.7 12.4 %collective-permute-start.19 = (bf16[16,2048]{1,0:T(8,128)(2,1)S(1)}, bf16[16,2048]{1,0:T(8,128)(2,1)S(1)}, u32[]{:S(2)}, u32[]{:S(2)}) collective-permute-start(bf16[16,2048]{1,0:T(8,128)(2,1)S(1)} %convolution_convert_fusion.1), channel_id=1, source_target_pairs={{0,24},{8,32},{16,40},{24,48},{32,56},{40,0},{48,8},{56,16},{1,25}... | collective-permute-start | bytes 196616 | tf_op jit(solution)/shard_map/ppermute | solution.py:52
  376.0 11.2 %collective-permute-start.20 = (bf16[16,2048]{1,0:T(8,128)(2,1)S(1)}, bf16[16,2048]{1,0:T(8,128)(2,1)S(1)}, u32[]{:S(2)}, u32[]{:S(2)}) collective-permute-start(bf16[16,2048]{1,0:T(8,128)(2,1)S(1)} %convolution_convert_fusion.1), channel_id=1, source_target_pairs={{0,32},{8,40},{16,48},{24,56},{32,0},{40,8},{48,16},{56,24},{1,33}... | collective-permute-start | bytes 196616 | tf_op jit(solution)/shard_map/ppermute | solution.py:52
  378.8 8.4 %collective-permute-start.21 = (bf16[16,2048]{1,0:T(8,128)(2,1)S(1)}, bf16[16,2048]{1,0:T(8,128)(2,1)S(1)}, u32[]{:S(2)}, u32[]{:S(2)}) collective-permute-start(bf16[16,2048]{1,0:T(8,128)(2,1)S(1)} %convolution_convert_fusion.1), channel_id=1, source_target_pairs={{0,40},{8,48},{16,56},{24,0},{32,8},{40,16},{48,24},{56,32},{1,41}... | collective-permute-start | bytes 196616 | tf_op jit(solution)/shard_map/ppermute | solution.py:52
  389.8 7.8 %collective-permute-start.24 = (bf16[16,512]{1,0:T(8,128)(2,1)S(1)}, bf16[16,512]{1,0:T(8,128)(2,1)S(1)}, u32[]{:S(2)}, u32[]{:S(2)}) collective-permute-start(bf16[16,512]{1,0:T(8,128)(2,1)S(1)} %convolution_convert_fusion.5), channel_id=1, source_target_pairs={{0,64},{64,128},{128,192},{192,0},{1,65},{65,129},{129,193},{193,1... | collective-permute-start | bytes 49160 | tf_op jit(solution)/shard_map/ppermute | solution.py:52
  391.2 7.8 %collective-permute-start.25 = (bf16[16,512]{1,0:T(8,128)(2,1)S(1)}, bf16[16,512]{1,0:T(8,128)(2,1)S(1)}, u32[]{:S(2)}, u32[]{:S(2)}) collective-permute-start(bf16[16,512]{1,0:T(8,128)(2,1)S(1)} %convolution_convert_fusion.5), channel_id=1, source_target_pairs={{0,128},{64,192},{128,0},{192,64},{1,129},{65,193},{129,1},{193,65... | collective-permute-start | bytes 49160 | tf_op jit(solution)/shard_map/ppermute | solution.py:52
  399.5 13.7 %collective-permute-start.27 = (bf16[16,2048]{1,0:T(8,128)(2,1)S(1)}, bf16[16,2048]{1,0:T(8,128)(2,1)S(1)}, u32[]{:S(2)}, u32[]{:S(2)}) collective-permute-start(bf16[16,2048]{1,0:T(8,128)(2,1)S(1)} %convolution_convert_fusion), channel_id=1, source_target_pairs={{0,8},{8,16},{16,24},{24,32},{32,40},{40,48},{48,56},{56,0},{1,9},... | collective-permute-start | bytes 196616 | tf_op jit(solution)/shard_map/ppermute | solution.py:52
  403.0 14.6 %collective-permute-start.28 = (bf16[16,2048]{1,0:T(8,128)(2,1)S(1)}, bf16[16,2048]{1,0:T(8,128)(2,1)S(1)}, u32[]{:S(2)}, u32[]{:S(2)}) collective-permute-start(bf16[16,2048]{1,0:T(8,128)(2,1)S(1)} %convolution_convert_fusion), channel_id=1, source_target_pairs={{0,16},{8,24},{16,32},{24,40},{32,48},{40,56},{48,0},{56,8},{1,17}... | collective-permute-start | bytes 196616 | tf_op jit(solution)/shard_map/ppermute | solution.py:52
  405.3 13.9 %collective-permute-start.29 = (bf16[16,2048]{1,0:T(8,128)(2,1)S(1)}, bf16[16,2048]{1,0:T(8,128)(2,1)S(1)}, u32[]{:S(2)}, u32[]{:S(2)}) collective-permute-start(bf16[16,2048]{1,0:T(8,128)(2,1)S(1)} %convolution_convert_fusion), channel_id=1, source_target_pairs={{0,24},{8,32},{16,40},{24,48},{32,56},{40,0},{48,8},{56,16},{1,25}... | collective-permute-start | bytes 196616 | tf_op jit(solution)/shard_map/ppermute | solution.py:52
  407.4 11.7 %collective-permute-start.30 = (bf16[16,2048]{1,0:T(8,128)(2,1)S(1)}, bf16[16,2048]{1,0:T(8,128)(2,1)S(1)}, u32[]{:S(2)}, u32[]{:S(2)}) collective-permute-start(bf16[16,2048]{1,0:T(8,128)(2,1)S(1)} %convolution_convert_fusion), channel_id=1, source_target_pairs={{0,32},{8,40},{16,48},{24,56},{32,0},{40,8},{48,16},{56,24},{1,33}... | collective-permute-start | bytes 196616 | tf_op jit(solution)/shard_map/ppermute | solution.py:52
  410.5 9.7 %collective-permute-start.31 = (bf16[16,2048]{1,0:T(8,128)(2,1)S(1)}, bf16[16,2048]{1,0:T(8,128)(2,1)S(1)}, u32[]{:S(2)}, u32[]{:S(2)}) collective-permute-start(bf16[16,2048]{1,0:T(8,128)(2,1)S(1)} %convolution_convert_fusion), channel_id=1, source_target_pairs={{0,40},{8,48},{16,56},{24,0},{32,8},{40,16},{48,24},{56,32},{1,41}... | collective-permute-start | bytes 196616 | tf_op jit(solution)/shard_map/ppermute | solution.py:52
  413.2 10.1 %collective-permute-start.32 = (bf16[16,2048]{1,0:T(8,128)(2,1)S(1)}, bf16[16,2048]{1,0:T(8,128)(2,1)S(1)}, u32[]{:S(2)}, u32[]{:S(2)}) collective-permute-start(bf16[16,2048]{1,0:T(8,128)(2,1)S(1)} %convolution_convert_fusion), channel_id=1, source_target_pairs={{0,48},{8,56},{16,0},{24,8},{32,16},{40,24},{48,32},{56,40},{1,49}... | collective-permute-start | bytes 196616 | tf_op jit(solution)/shard_map/ppermute | solution.py:52
  (25 other events, 467.8 us)
Sparse Core Ops, SparseCore 0:
  21.5 29.4 all-gather.14
  52.7 55.1 all-gather.16
  109.8 24.4 all-gather.12
  223.1 21.3 all-gather.18
  355.6 30.2 reduce-scatter.6
  403.1 19.0 reduce-scatter.4
